TPU v7x, 32 devices: a whole 2x2x4 slice. The times are simulated.
32 devices in a mesh: grp: 2 (over y), seq: 4 (over z), batch: 4 (over x, core).
Axes of the slice: x: 2, y: 2, z: 4, core: 2. Of those that a mesh axis runs over, the one named last changes fastest.
Arguments:
- head_split_gradient: bfloat16 [8, 768, 2048], P(('grp', 'batch'), 'seq'), parts along dimension 0, may hold values from -6 to 6
- first_layer_input: bfloat16 [8, 768, 2048], P(('grp', 'batch'), None, 'seq'), parts along dimension 0, may hold values from -40 to 40
- second_layer_input: bfloat16 [8, 768, 2048], P(('grp', 'batch'), None, 'seq'), parts along dimension 0, may hold values from -40 to 40
- first_layer_weight: bfloat16 [3, 768, 768], replicated, may hold values from -0.125 to 0.125
- second_layer_weight: bfloat16 [3, 768, 768], replicated, may hold values from -0.125 to 0.125
- first_norm_gain: float32 [768], replicated, may hold values from 0.1 to 1.9
- second_norm_gain: float32 [768], replicated, may hold values from 0.1 to 1.9
Outputs:
- input_gradient_total: bfloat16 [8, 768, 2048], P(('grp', 'batch'), None, 'seq'), parts along dimension 0
- first_weight_gradient: float32 [4608, 768], P(('grp', 'seq')), parts along dimension 0
There are 2 independent parts, one for each index of `grp`. A program takes and returns all parts, laid end to end along the dimension named above; an argument that names none is the same for every part. Nothing has to cross between parts.
All inputs are finite; a program needn't handle non-finite values.
Results may differ from a plain program's by a relative error of at most 0.005.
Values may be sent and summed in bfloat16 or wider, within the bound.
A program may use at most 64 MiB of HBM per device.

v0:
```python
import math

import jax
import jax.numpy as jnp
from jax import lax
from jax.sharding import PartitionSpec as P

DILATION_FIRST = 512
DILATION_SECOND = 1024


EPS = 1e-06
SLOPE = math.sqrt(2.0 / math.pi)
CUBIC = 0.044715


def shifted(value, axis, steps):
    count = lax.axis_size(axis)
    initial, last = (max(0, -steps), min(count, count - steps))
    return lax.ppermute(value, axis, [(source, source + steps) for source in range(initial, last)])


def gelu_slope(normed):
    inner = jnp.tanh(SLOPE * (normed + CUBIC * normed * normed * normed))
    return 0.5 * (1.0 + inner) + 0.5 * normed * (1.0 - inner * inner) * SLOPE * (
        1.0 + 3.0 * CUBIC * normed * normed
    )


def prepare(inputs, gain_vec):
    xfloat = inputs.astype(jnp.float32)
    meansq = jnp.mean(xfloat * xfloat, axis=1, keepdims=True)
    scale = lax.rsqrt(meansq + EPS)
    normed = xfloat * scale * gain_vec[None, :, None]
    gelu_out = jax.nn.gelu(normed, approximate=True).astype(jnp.bfloat16)
    return (xfloat, scale, normed, gelu_out)


def border_rows(grad_out, shard_span):
    lower_grad = shifted(grad_out, "seq", shard_span)
    upper_grad = shifted(grad_out, "seq", -shard_span)
    return (lower_grad, upper_grad)


def input_grad(xfloat, scale, normed, gain_vec, weight, grad_out, grad_upper, grad_lower):
    dgelu = jnp.einsum("co,sop->scp", weight[0], grad_upper, preferred_element_type=jnp.float32)
    dgelu = dgelu + jnp.einsum(
        "co,sop->scp", weight[1], grad_out, preferred_element_type=jnp.float32
    )
    dgelu = dgelu + jnp.einsum(
        "co,sop->scp", weight[2], grad_lower, preferred_element_type=jnp.float32
    )
    dnorm = dgelu * gelu_slope(normed) * gain_vec[None, :, None]
    inner = jnp.mean(dnorm * xfloat, axis=1, keepdims=True)
    dinput = scale * dnorm - xfloat * scale * scale * scale * inner
    return (grad_out.astype(jnp.float32) + dinput).astype(jnp.bfloat16)


def local_terms(gelu_out, grad_upper, grad_out, grad_lower, scale_factor):
    pieces = [
        jnp.einsum("scp,sop->co", gelu_out, tapped, preferred_element_type=jnp.float32)
        for tapped in (grad_upper, grad_out, grad_lower)
    ]
    return jnp.concatenate(pieces, axis=0) * scale_factor


def on_device(
    head_split_gradient,
    first_layer_input,
    second_layer_input,
    first_layer_weight,
    second_layer_weight,
    first_norm_gain,
    second_norm_gain,
):
    second_layer_gradient = lax.all_to_all(
        head_split_gradient, "seq", split_axis=2, concat_axis=1, tiled=True
    )
    border_width = first_layer_input.shape[2]
    scale_factor = 1.0 / math.sqrt(
        first_layer_input.shape[0] * lax.axis_size("batch") * border_width * lax.axis_size("seq")
    )
    xfloat_two, scale_two, normed_two, gelu_two = prepare(second_layer_input, second_norm_gain)
    second_lower_border, second_upper_border = border_rows(
        second_layer_gradient, DILATION_SECOND // border_width
    )
    middle_gradient = input_grad(
        xfloat_two,
        scale_two,
        normed_two,
        second_norm_gain,
        second_layer_weight,
        second_layer_gradient,
        second_upper_border,
        second_lower_border,
    )
    xfloat_one, scale_one, normed_one, gelu_one = prepare(first_layer_input, first_norm_gain)
    first_lower_border, first_upper_border = border_rows(
        middle_gradient, DILATION_FIRST // border_width
    )
    input_gradient_total = input_grad(
        xfloat_one,
        scale_one,
        normed_one,
        first_norm_gain,
        first_layer_weight,
        middle_gradient,
        first_upper_border,
        first_lower_border,
    )
    terms_one = local_terms(
        gelu_one, first_upper_border, middle_gradient, first_lower_border, scale_factor
    )
    partial_rows = lax.psum_scatter(terms_one, "seq", scatter_dimension=0, tiled=True)
    first_weight_gradient = lax.psum(partial_rows, "batch")
    return (input_gradient_total, first_weight_gradient)


def solution(mesh):
    in_specs = (
        P(("grp", "batch"), "seq", None),
        P(("grp", "batch"), None, "seq"),
        P(("grp", "batch"), None, "seq"),
        P(),
        P(),
        P(),
        P(),
    )
    out_specs = (P(("grp", "batch"), None, "seq"), P(("grp", "seq"), None))
    return jax.shard_map(
        on_device, mesh=mesh, in_specs=in_specs, out_specs=out_specs, check_vma=False
    )
```

profile of v0, /device:TPU:1, one launch (start us, length us, event | category | flops | bytes accessed | tf_op | source)
XLA Modules:
  0.0 307.0 jit_solution(13687782460259518762)
XLA Ops:
  7.2 0.0 reduce-scatter.2.cloned.1.call-start
  7.2 4.5 %copy.23 = bf16[1,192,2048]{1,0,2:T(2,128)(2,1)S(1)} copy(bf16[1,192,2048]{2,1,0:T(8,128)(2,1)} %param.7) | data formatting | bytes 1572864 | tf_op args[0]
  11.8 0.5 broadcast.102
  12.3 11.6 %reduce.4 = bf16[2048,192]{1,0:T(8,128)(2,1)S(1)} reduce(bf16[2048,1,192]{2,1,0:T(2,128)(2,1)S(1)} %bitcast.70, bf16[]{:T(256)} %broadcast.102), dimensions={1}, to_apply=%bitcast.59.reduce_sub_computation | reduce | bytes 1572866
  23.9 1.4 reshape.110
  25.3 24.5 %all_to_all.18 = bf16[4,2,49152]{2,1,0:T(2,128)(2,1)S(1)} all-to-all(bf16[4,2,49152]{2,1,0:T(2,128)(2,1)S(1)} %reshape.110), channel_id=1, replica_groups=mesh['grp'=2,'seq'=4,'batch'=4] {'seq'}, dimensions={0} | all-to-all | bytes 1572864 | tf_op jit(solution)/shard_map/all_to_all | solution.py:76
  49.8 1.4 reshape.111
  51.1 1.2 copy.24
  52.4 0.6 all_to_all.14
  52.9 0.0 copy-start
  53.0 0.1 copy.25
  53.1 1.4 collective-permute-start
  54.5 0.3 copy.27
  54.8 0.2 fusion.35
  55.1 5.8 %collective-permute-start.1 = (bf16[1,768,512]{2,1,0:T(8,128)(2,1)S(1)}, bf16[1,768,512]{2,1,0:T(8,128)(2,1)S(1)}, u32[]{:S(2)}, u32[]{:S(2)}) collective-permute-start(bf16[1,768,512]{2,1,0:T(8,128)(2,1)S(1)} %bitcast.73), channel_id=1, source_target_pairs={{0,8},{4,12},{1,9},{5,13},{2,10},{6,14},{3,11},{7,15},{16,24},{20,... | collective-permute-start | bytes 2359304 | tf_op jit(solution)/shard_map/ppermute | solution.py:20
  60.9 0.3 copy.26
  61.1 0.0 copy-start.2
  61.2 2.2 fusion.58
  63.4 0.0 copy-start.3
  63.4 28.3 %collective-permute-done = bf16[1,768,512]{2,1,0:T(8,128)(2,1)} collective-permute-done((bf16[1,768,512]{2,1,0:T(8,128)(2,1)S(1)}, bf16[1,768,512]{2,1,0:T(8,128)(2,1)}, u32[]{:S(2)}, u32[]{:S(2)}) %collective-permute-start) | collective-permute-done | bytes 786464 | tf_op jit(solution)/shard_map/ppermute | solution.py:20
  91.7 2.0 fusion.60
  93.7 0.0 collective-permute-done.1
  93.7 2.3 fusion.36
  96.0 0.0 copy-start.1
  96.0 0.6 fusion.34
  96.6 0.0 copy-start.4
  96.6 1.3 collective-permute-start.2
  97.9 0.0 copy-done.1
  97.9 0.3 copy.29
  98.2 0.2 fusion.40
  98.4 4.2 %collective-permute-start.3 = (bf16[1,768,512]{1,2,0:T(8,128)(2,1)S(1)}, bf16[1,768,512]{1,2,0:T(8,128)(2,1)S(1)}, u32[]{:S(2)}, u32[]{:S(2)}) collective-permute-start(bf16[1,768,512]{1,2,0:T(8,128)(2,1)S(1)} %fusion.34), channel_id=1, source_target_pairs={{0,4},{4,8},{8,12},{1,5},{5,9},{9,13},{2,6},{6,10},{10,14},{3,7},{... | collective-permute-start | bytes 2359304 | tf_op jit(solution)/shard_map/ppermute | solution.py:20
  102.7 1.2 fusion.72
  103.9 13.3 %collective-permute-done.2 = bf16[1,768,512]{1,2,0:T(8,128)(2,1)} collective-permute-done((bf16[1,768,512]{1,2,0:T(8,128)(2,1)S(1)}, bf16[1,768,512]{1,2,0:T(8,128)(2,1)}, u32[]{:S(2)}, u32[]{:S(2)}) %collective-permute-start.2) | collective-permute-done | bytes 786464 | tf_op jit(solution)/shard_map/ppermute | solution.py:20
  117.2 2.3 fusion.75
  119.6 0.0 collective-permute-done.3
  119.6 1.2 fusion.69
  120.8 3.3 %maximum_multiply_fusion = f32[2304,768]{1,0:T(8,128)} fusion(f32[768,768]{1,0:T(8,128)S(1)} %fusion.69, f32[768,768]{1,0:T(8,128)S(1)} %fusion.72, f32[768,768]{1,0:T(8,128)S(1)} %fusion.75), kind=kLoop, calls=%fused_computation | loop fusion | flops 5308416 | bytes 14155776 | tf_op jit(solution)/shard_map/mul | solution.py:64
  124.1 0.0 reduce-scatter.2.cloned.1.call-update
  124.1 0.0 all-reduce.2.cloned.1.call-start
  124.2 3.3 %fusion.50 = f32[512,768]{1,0:T(8,128)} fusion(bf16[3,768,768]{2,1,0:T(8,128)(2,1)} %param.10, bf16[1,768,512]{1,2,0:T(8,128)(2,1)S(1)} %fusion.34), kind=kOutput, calls=%fused_computation.60 | convolution fusion | flops 603979776 | bytes 3538944 | tf_op jit(solution)/shard_map/co,sop->scp/dot_general | solution.py:47
  127.4 3.5 %fusion.52 = f32[512,768]{1,0:T(8,128)} fusion(bf16[3,768,768]{2,1,0:T(8,128)(2,1)} %param.10, bf16[1,768,512]{1,2,0:T(8,128)(2,1)} %collective-permute-done.2), kind=kOutput, calls=%fused_computation.62 | convolution fusion | flops 603979776 | bytes 3538944 | tf_op jit(solution)/shard_map/co,sop->scp/dot_general | solution.py:46
  130.9 117.6 %reduce-scatter.2.cloned.1.call-done = f32[576,768]{1,0:T(8,128)} async-done(((f32[2304,768]{1,0:T(8,128)}), f32[576,768]{1,0:T(8,128)}) %reduce-scatter.2.cloned.1.call-update) | async-done | bytes 1769488 | tf_op jit(solution)/shard_map/reduce_scatter | solution.py:114
  248.5 0.0 all-reduce.2.cloned.1.call-update
  248.6 4.2 %fusion.41 = (f32[512]{0:T(512)S(1)}, f32[1,768,512]{1,2,0:T(8,128)S(1)}) fusion(bf16[1,768,512]{1,2,0:T(8,128)(2,1)S(1)} %copy.29, f32[768]{0:T(1024)S(1)} %copy-done.4, f32[512]{0:T(512)S(1)} %add_rsqrt_fusion, bf16[3,768,768]{2,1,0:T(8,128)(2,1)} %param.10, bf16[1,768,512]{1,2,0:T(8,128)(2,1)S(1)} %collective-permute-done.3, f32[512,768]{1,0:T(8,128)} %fusion.52, ...), kind=kOutput, calls=%fused_computation.53 | convolution fusion | flops 614202880 | bytes 7478272 | tf_op jit(solution)/shard_map/co,sop->scp/dot_general | solution.py:50
  252.7 0.6 fusion.23
  253.3 1.2 copy.30
  254.5 42.9 %all-reduce.2.cloned.1.call-done = f32[576,768]{1,0:T(8,128)} async-done(((f32[576,768]{1,0:T(8,128)}), f32[576,768]{1,0:T(8,128)}) %all-reduce.2.cloned.1.call-update) | async-done | bytes 1769488 | tf_op jit(solution)/shard_map/psum | solution.py:115
  297.4 2.8 copy.32
  (8 shorter events, 0.0 us)
Async XLA Ops:
  7.2 241.4 %reduce-scatter.2.cloned.1.call-start = ((), (), s32[]{:S(2)}) async-start(), calls=%async_computation.2 | async-start | bytes 8847360 | tf_op jit(solution)/shard_map/reduce_scatter | solution.py:114
  52.9 1.6 copy-start
  53.1 38.6 %collective-permute-start = (bf16[1,768,512]{2,1,0:T(8,128)(2,1)S(1)}, bf16[1,768,512]{2,1,0:T(8,128)(2,1)}, u32[]{:S(2)}, u32[]{:S(2)}) collective-permute-start(bf16[1,768,512]{2,1,0:T(8,128)(2,1)S(1)} %bitcast.72), channel_id=1, source_target_pairs={{8,0},{12,4},{9,1},{13,5},{10,2},{14,6},{11,3},{15,7},{24,16},{28,... | collective-permute-start | bytes 2359304 | tf_op jit(solution)/shard_map/ppermute | solution.py:20
  55.1 38.7 %collective-permute-start.1 = (bf16[1,768,512]{2,1,0:T(8,128)(2,1)S(1)}, bf16[1,768,512]{2,1,0:T(8,128)(2,1)S(1)}, u32[]{:S(2)}, u32[]{:S(2)}) collective-permute-start(bf16[1,768,512]{2,1,0:T(8,128)(2,1)S(1)} %bitcast.73), channel_id=1, source_target_pairs={{0,8},{4,12},{1,9},{5,13},{2,10},{6,14},{3,11},{7,15},{16,24},{20,... | collective-permute-start | bytes 2359304 | tf_op jit(solution)/shard_map/ppermute | solution.py:20
  61.1 30.6 %copy-start.2 = (bf16[3,768,768]{2,1,0:T(8,128)(2,1)S(1)}, bf16[3,768,768]{2,1,0:T(8,128)(2,1)}, u32[]{:S(2)}) copy-start(bf16[3,768,768]{2,1,0:T(8,128)(2,1)} %param.11) | copy-start | bytes 10616836
  63.4 30.3 %copy-start.3 = (f32[768]{0:T(1024)S(1)}, f32[768]{0:T(1024)}, u32[]{:S(2)}) copy-start(f32[768]{0:T(1024)} %param.13) | copy-start | bytes 9220
  96.0 1.9 copy-start.1
  96.6 6.1 %copy-start.4 = (f32[768]{0:T(1024)S(1)}, f32[768]{0:T(1024)}, u32[]{:S(2)}) copy-start(f32[768]{0:T(1024)} %param.12) | copy-start | bytes 9220
  96.6 20.6 %collective-permute-start.2 = (bf16[1,768,512]{1,2,0:T(8,128)(2,1)S(1)}, bf16[1,768,512]{1,2,0:T(8,128)(2,1)}, u32[]{:S(2)}, u32[]{:S(2)}) collective-permute-start(bf16[1,768,512]{1,2,0:T(8,128)(2,1)S(1)} %fusion.34), channel_id=1, source_target_pairs={{4,0},{8,4},{12,8},{5,1},{9,5},{13,9},{6,2},{10,6},{14,10},{7,3},{... | collective-permute-start | bytes 2359304 | tf_op jit(solution)/shard_map/ppermute | solution.py:20
  98.4 21.2 %collective-permute-start.3 = (bf16[1,768,512]{1,2,0:T(8,128)(2,1)S(1)}, bf16[1,768,512]{1,2,0:T(8,128)(2,1)S(1)}, u32[]{:S(2)}, u32[]{:S(2)}) collective-permute-start(bf16[1,768,512]{1,2,0:T(8,128)(2,1)S(1)} %fusion.34), channel_id=1, source_target_pairs={{0,4},{4,8},{8,12},{1,5},{5,9},{9,13},{2,6},{6,10},{10,14},{3,7},{... | collective-permute-start | bytes 2359304 | tf_op jit(solution)/shard_map/ppermute | solution.py:20
  124.1 173.3 %all-reduce.2.cloned.1.call-start = ((), (), s32[]{:S(2)}) async-start(), calls=%async_computation.3 | async-start | bytes 3538944 | tf_op jit(solution)/shard_map/psum | solution.py:115
Sparse Core Ops, SparseCore 0:
  124.2 124.2 reduce-scatter.1
  250.9 46.4 all-reduce.1
where the time goes:
time: 308 us; the launch traced here: 307 us
  waiting for transfers between devices  202 us (66%)
  blocking collectives  24.5 us (8%)
  matrix products  22.2 us (7%)
  other arithmetic  16.5 us (5%)
  local copies, waits for them, and re-layouts  14.5 us (5%)
  between operations  14.3 us (5%)
  starting transfers between devices  12.8 us (4%)
    reduce_scatter x1, waiting for transfers between devices, on_device(): lax.psum_scatter(terms_one, 'seq', scatter_dimension=0, tiled=True)  118 us
    psum x1, waiting for transfers between devices, on_device(): first_weight_gradient = lax.psum(partial_rows, 'batch')  42.9 us
    ppermute x4, waiting for transfers between devices, shifted(): lax.ppermute(value, axis, [(source, source + steps) for source in range(i...  41.7 us
    all_to_all x1, blocking collectives, on_device(): lax.all_to_all(head_split_gradient, 'seq', split_axis=2, concat_axis=1, t...  24.5 us
    ppermute x4, starting transfers between devices, shifted(): lax.ppermute(value, axis, [(source, source + steps) for source in range(i...  12.7 us
    unnamed x18, local copies, waits for them, and re-layouts  12.3 us
    unnamed x1, other arithmetic  11.6 us
    dot_general x2, matrix products, input_grad(): jnp.einsum('co,sop->scp', weight[2], grad_lower, preferred_element_type=j...  6.43 us
  transfers between devices with their start and end apart: 6, of which 4 were waited for; matrix products, arithmetic and copies ran while one was open for 7% of the time, Pallas kernels for 0%

commit v1 on v0

v1 whole, which is shorter than its diff:
```python
import functools
import math

import jax
import jax.numpy as jnp
from jax import lax
from jax.experimental import pallas as pl
from jax.experimental.pallas import tpu as pltpu
from jax.sharding import PartitionSpec as P

DILATION_FIRST = 512
DILATION_SECOND = 1024

EPS = 1e-06
SLOPE = math.sqrt(2.0 / math.pi)
CUBIC = 0.044715

F32 = jnp.float32
BF16 = jnp.bfloat16
MESH = pl.DeviceIdType.MESH
CHUNKS = 2
STRIP = 64
BLOCK = 256


def prepare(u_ref, gain_ref, slope_ref, scale_ref, gelu_ref):
    chan, width = u_ref.shape

    def square(step, total):
        rows = pl.ds(pl.multiple_of(step * STRIP, STRIP), STRIP)
        x = u_ref[rows, :].astype(F32)
        return total + jnp.sum(x * x, axis=0, keepdims=True)

    total = lax.fori_loop(0, chan // STRIP, square, jnp.zeros((1, width), F32))
    scale = lax.rsqrt(total / chan + EPS)
    scale_ref[...] = scale

    @pl.loop(0, chan // STRIP)
    def _(step):
        rows = pl.ds(pl.multiple_of(step * STRIP, STRIP), STRIP)
        gain = gain_ref[rows, :]
        a = u_ref[rows, :].astype(F32) * scale * gain
        t = jnp.tanh(SLOPE * (a + CUBIC * a * a * a))
        slope = 0.5 * (1.0 + t) + 0.5 * a * (1.0 - t * t) * SLOPE * (1.0 + 3.0 * CUBIC * a * a)
        slope_ref[rows, :] = slope * gain
        if gelu_ref is not None:
            gelu_ref[rows, :] = (0.5 * a * (1.0 + t)).astype(BF16)


def layer(w_ref, e_ref, has_low, has_up, cols, u_ref, slope_ref, scale_ref, dg_ref, store):
    chan = u_ref.shape[0]
    width = cols.size

    def taps(tap, side, add):
        @pl.loop(0, chan // BLOCK)
        def _(step):
            rows = pl.ds(pl.multiple_of(step * BLOCK, BLOCK), BLOCK)
            part = jnp.dot(w_ref[tap, rows, :], e_ref[side, :, cols], preferred_element_type=F32)
            dg_ref[rows, :] = dg_ref[rows, :] + part if add else part

    taps(1, 1, False)

    @pl.when(has_low)
    def _():
        taps(2, 0, True)

    @pl.when(has_up)
    def _():
        taps(0, 2, True)

    def inner_step(step, total):
        rows = pl.ds(pl.multiple_of(step * STRIP, STRIP), STRIP)
        dn = dg_ref[rows, :] * slope_ref[rows, cols]
        dg_ref[rows, :] = dn
        return total + jnp.sum(dn * u_ref[rows, cols].astype(F32), axis=0, keepdims=True)

    inner = lax.fori_loop(0, chan // STRIP, inner_step, jnp.zeros((1, width), F32)) / chan
    scale = scale_ref[:, cols]
    cubed = scale * scale * scale * inner

    @pl.loop(0, chan // STRIP)
    def _(step):
        rows = pl.ds(pl.multiple_of(step * STRIP, STRIP), STRIP)
        dinput = scale * dg_ref[rows, :] - u_ref[rows, cols].astype(F32) * cubed
        store(rows, (e_ref[1, rows, cols].astype(F32) + dinput).astype(BF16))


def kernel(
    count, spans, factor, reduce,
    h_ref, u1_ref, u2_ref, w1_hbm, w2_hbm, c1_ref, c2_ref,
    grad_ref, wgrad_ref,
    w1, w2, e, m, slope1, slope2, scale1, scale2, gelu1, dg, terms,
    w_sem, a_send, a_recv, b_send, b_recv, *more,
):
    span_first, span_second = spans
    z = lax.axis_index("seq")
    chan, width = u1_ref.shape
    share = h_ref.shape[0]
    piece = width // CHUNKS

    load2 = pltpu.make_async_copy(w2_hbm, w2, w_sem.at[0])
    load1 = pltpu.make_async_copy(w1_hbm, w1, w_sem.at[1])
    load2.start()
    load1.start()

    offsets = sorted(range(1, count), key=lambda j: -min(j, count - j))
    barrier = pltpu.get_barrier_semaphore()
    partners = [{"seq": lax.rem(z + j, count)} for j in offsets]
    if reduce:
        b = lax.axis_index("batch")
        x, core = b // 2, b % 2
        sib, across = x * 2 + 1 - core, (1 - x) * 2 + core
        partners += [{"batch": sib}, {"batch": across}]
    for partner in partners:
        pl.semaphore_signal(barrier, inc=1, device_id=partner, device_id_type=MESH)
    pl.semaphore_wait(barrier, len(partners))

    def valid(side, owner, span):
        if side == 0:
            return owner >= span
        return owner + span < count

    def share_copy(q, j, side, source, dest):
        shift = (side - 1) * span_second
        at = pl.multiple_of((dest + shift) * width, 128) + q * piece
        return pltpu.make_async_remote_copy(
            src_ref=h_ref.at[:, pl.ds(pl.multiple_of(at, 128), piece)],
            dst_ref=e.at[side, pl.ds(pl.multiple_of(source * share, 16), share), pl.ds(q * piece, piece)],
            send_sem=a_send.at[q, j - 1, side],
            recv_sem=a_recv.at[q, j - 1, side],
            device_id={"seq": dest},
            device_id_type=MESH,
        )

    def each_share(q, act, incoming):
        for j in offsets:
            source = lax.rem(z - j + count, count) if incoming else z
            dest = z if incoming else lax.rem(z + j, count)
            for side in (0, 1, 2):
                def go(side=side):
                    act(share_copy(q, j, side, source, dest))
                if side == 1:
                    go()
                else:
                    pl.when(valid(side, dest, span_second))(go)

    for q in range(CHUNKS):
        each_share(q, lambda copy: copy.start(), False)

    own = pl.ds(pl.multiple_of(z * share, 16), share)
    for side in (0, 1, 2):
        def keep(side=side):
            at = pl.multiple_of((z + (side - 1) * span_second) * width, 128)
            e[side, own, :] = h_ref[:, pl.ds(at, width)]
        if side == 1:
            keep()
        else:
            pl.when(valid(side, z, span_second))(keep)

    prepare(u2_ref, c2_ref, slope2, scale2, None)
    prepare(u1_ref, c1_ref, slope1, scale1, gelu1)
    load2.wait()

    def border_copy(q, side):
        to = z + span_first if side == 0 else z - span_first
        cols = pl.ds(q * piece, piece)
        return pltpu.make_async_remote_copy(
            src_ref=m.at[1, :, cols],
            dst_ref=m.at[side, :, cols],
            send_sem=b_send.at[q, side // 2],
            recv_sem=b_recv.at[q, side // 2],
            device_id={"seq": to},
            device_id_type=MESH,
        )

    sends_up = z + span_first < count
    sends_down = z >= span_first

    for q in range(CHUNKS):
        each_share(q, lambda copy: copy.wait_recv(), True)
        cols = pl.ds(q * piece, piece)

        def store_middle(rows, value):
            m[1, rows, cols] = value

        layer(
            w2, e, valid(0, z, span_second), valid(2, z, span_second), cols,
            u2_ref, slope2, scale2, dg, store_middle,
        )

        @pl.when(sends_up)
        def _():
            border_copy(q, 0).start()

        @pl.when(sends_down)
        def _():
            border_copy(q, 2).start()

    def tap_terms(tap, side):
        @pl.loop(0, chan // BLOCK)
        def _(step):
            start = pl.multiple_of(step * BLOCK, BLOCK)
            part = lax.dot_general(
                gelu1[pl.ds(start, BLOCK), :], m[side],
                (((1,), (1,)), ((), ())), preferred_element_type=F32,
            )
            terms[pl.ds(pl.multiple_of(tap * chan + start, BLOCK), BLOCK), :] = part * factor

    def border_terms(tap, side, has):
        @pl.when(has)
        def _():
            for q in range(CHUNKS):
                border_copy(q, side).wait_recv()
            tap_terms(tap, side)

        @pl.when(jnp.logical_not(has))
        def _():
            terms[pl.ds(tap * chan, chan), :] = jnp.zeros((chan, terms.shape[1]), F32)

    tap_terms(1, 1)
    border_terms(0, 2, sends_up)
    border_terms(2, 0, sends_down)
    load1.wait()

    def store_total(cols):
        def store(rows, value):
            grad_ref[rows, cols] = value
        return store

    def first_layer():
        for q in range(CHUNKS):
            cols = pl.ds(q * piece, piece)
            layer(
                w1, m, sends_down, sends_up, cols,
                u1_ref, slope1, scale1, dg, store_total(cols),
            )

    if reduce:
        reduce_terms(count, z, x, core, sib, across, terms, wgrad_ref, first_layer, *more)
    else:
        first_layer()
        wgrad_ref[...] = terms[...]

    for q in range(CHUNKS):
        each_share(q, lambda copy: copy.wait_send(), False)

        @pl.when(sends_up)
        def _():
            border_copy(q, 0).wait_send()

        @pl.when(sends_down)
        def _():
            border_copy(q, 2).wait_send()


def reduce_terms(
    count, z, x, core, sib, across, terms, wgrad_ref, meanwhile,
    core_out, core_in, x_out, x_in, z_out, z_in, kept, final,
    core_send, core_recv, x_send, x_recv, z_send, z_recv, f_send, f_recv,
):
    rows_each, half = core_out.shape[1:]
    order = sorted(range(count), key=lambda j: (j == 0, -min(j, count - j)))

    def rows_of(j, part):
        block = lax.rem(z + j, count)
        return pl.ds(pl.multiple_of(block * (2 * rows_each) + part * rows_each, 16), rows_each)

    mine = pl.ds(pl.multiple_of(core * half, 128), half)
    theirs = pl.ds(pl.multiple_of((1 - core) * half, 128), half)

    def core_copy(slot):
        return pltpu.make_async_remote_copy(
            src_ref=core_out.at[slot], dst_ref=core_in.at[slot],
            send_sem=core_send.at[slot], recv_sem=core_recv.at[slot],
            device_id={"batch": sib}, device_id_type=MESH,
        )

    def x_copy(j):
        return pltpu.make_async_remote_copy(
            src_ref=x_out.at[j], dst_ref=x_in.at[j],
            send_sem=x_send.at[j], recv_sem=x_recv.at[j],
            device_id={"batch": across}, device_id_type=MESH,
        )

    def z_copy(j, dest):
        return pltpu.make_async_remote_copy(
            src_ref=z_out.at[j - 1], dst_ref=z_in.at[j - 1],
            send_sem=z_send.at[j - 1], recv_sem=z_recv.at[j - 1],
            device_id={"seq": dest}, device_id_type=MESH,
        )

    for group, part in ((0, 1 - x), (1, x)):
        for j in order:
            slot = group * count + j
            core_out[slot] = terms[rows_of(j, part), theirs].astype(BF16)
            core_copy(slot).start()
    for j in order:
        core_copy(j).wait_recv()
        x_out[j] = (terms[rows_of(j, 1 - x), mine] + core_in[j].astype(F32)).astype(BF16)
        x_copy(j).start()

    meanwhile()

    for j in order:
        core_copy(count + j).wait_recv()
        x_copy(j).wait_recv()
        total = terms[rows_of(j, x), mine] + core_in[count + j].astype(F32) + x_in[j].astype(F32)
        if j == 0:
            kept[...] = total
        else:
            z_out[j - 1] = total.astype(BF16)
            z_copy(j, lax.rem(z + j, count)).start()
    for j in order[:-1]:
        z_copy(j, lax.rem(z + j, count)).wait_recv()
        kept[...] += z_in[j - 1].astype(F32)

    me = x * 2 + core
    final[me] = kept[...].astype(BF16)

    def final_copy(index, slot, to):
        return pltpu.make_async_remote_copy(
            src_ref=final.at[slot], dst_ref=final.at[slot],
            send_sem=f_send.at[index], recv_sem=f_recv.at[index],
            device_id={"batch": to}, device_id_type=MESH,
        )

    final_copy(0, me, across).start()
    final_copy(1, me, sib).start()
    final_copy(0, across, across).wait_recv()
    final_copy(2, across, sib).start()
    final_copy(1, sib, sib).wait_recv()
    final_copy(2, (1 - x) * 2 + 1 - core, sib).wait_recv()
    for part in range(2):
        for side in range(2):
            wgrad_ref[pl.ds(part * rows_each, rows_each), pl.ds(side * half, half)] = final[
                part * 2 + side
            ].astype(F32)

    final_copy(0, me, across).wait_send()
    final_copy(1, me, sib).wait_send()
    final_copy(2, across, sib).wait_send()
    for slot in range(2 * count):
        core_copy(slot).wait_send()
    for j in range(count):
        x_copy(j).wait_send()
    for j in range(1, count):
        z_copy(j, lax.rem(z + j, count)).wait_send()


def on_device(seq, batch, head, u1, u2, w1, w2, c1, c2):
    chan, width = u1.shape[1:]
    out_chan = w1.shape[2]
    taps = w1.shape[0]
    total_rows = taps * chan
    factor = 1.0 / math.sqrt(u1.shape[0] * batch * width * seq)
    spans = (DILATION_FIRST // width, DILATION_SECOND // width)
    rows = total_rows // seq
    reduce = batch == 4 and rows % 32 == 0 and out_chan % 256 == 0
    rows_each, half = rows // 2, out_chan // 2
    vmem = pl.BlockSpec(memory_space=pltpu.VMEM)
    anywhere = pl.BlockSpec(memory_space=pl.ANY)
    dma = pltpu.SemaphoreType.DMA
    scratch = [
        pltpu.VMEM(w1.shape, BF16),
        pltpu.VMEM(w2.shape, BF16),
        pltpu.VMEM((3, chan, width), BF16),
        pltpu.VMEM((3, chan, width), BF16),
        pltpu.VMEM((chan, width), F32),
        pltpu.VMEM((chan, width), F32),
        pltpu.VMEM((1, width), F32),
        pltpu.VMEM((1, width), F32),
        pltpu.VMEM((chan, width), BF16),
        pltpu.VMEM((chan, width // CHUNKS), F32),
        pltpu.VMEM((total_rows, out_chan), F32),
        dma((2,)),
        dma((CHUNKS, seq - 1, 3)),
        dma((CHUNKS, seq - 1, 3)),
        dma((CHUNKS, 2)),
        dma((CHUNKS, 2)),
    ]
    if reduce:
        scratch += [
            pltpu.VMEM((2 * seq, rows_each, half), BF16),
            pltpu.VMEM((2 * seq, rows_each, half), BF16),
            pltpu.VMEM((seq, rows_each, half), BF16),
            pltpu.VMEM((seq, rows_each, half), BF16),
            pltpu.VMEM((seq - 1, rows_each, half), BF16),
            pltpu.VMEM((seq - 1, rows_each, half), BF16),
            pltpu.VMEM((rows_each, half), F32),
            pltpu.VMEM((4, rows_each, half), BF16),
            dma((2 * seq,)),
            dma((2 * seq,)),
            dma((seq,)),
            dma((seq,)),
            dma((seq - 1,)),
            dma((seq - 1,)),
            dma((3,)),
            dma((3,)),
        ]
    grad, wgrad = pl.pallas_call(
        functools.partial(kernel, seq, spans, factor, reduce),
        out_shape=(
            jax.ShapeDtypeStruct((chan, width), BF16),
            jax.ShapeDtypeStruct((rows if reduce else total_rows, out_chan), F32),
        ),
        in_specs=[vmem, vmem, vmem, anywhere, anywhere, vmem, vmem],
        out_specs=(vmem, vmem),
        scratch_shapes=scratch,
        compiler_params=pltpu.CompilerParams(
            collective_id=0, has_side_effects=True, vmem_limit_bytes=56 * 1024 * 1024
        ),
        cost_estimate=pl.CostEstimate(
            flops=18 * chan * out_chan * width, bytes_accessed=20_000_000, transcendentals=2 * chan * width
        ),
    )(head[0], u1[0], u2[0], w1, w2, c1.reshape(chan, 1), c2.reshape(chan, 1))
    if not reduce:
        wgrad = lax.psum(lax.psum_scatter(wgrad, "seq", scatter_dimension=0, tiled=True), "batch")
    return grad[None], wgrad


def solution(mesh):
    in_specs = (
        P(("grp", "batch"), "seq", None),
        P(("grp", "batch"), None, "seq"),
        P(("grp", "batch"), None, "seq"),
        P(),
        P(),
        P(),
        P(),
    )
    out_specs = (P(("grp", "batch"), None, "seq"), P(("grp", "seq"), None))
    return jax.shard_map(
        functools.partial(on_device, mesh.shape["seq"], mesh.shape["batch"]),
        mesh=mesh, in_specs=in_specs, out_specs=out_specs, check_vma=False,
    )
```

time: 308 us -> 104 us (0.34)
  waiting for transfers between devices: 202 us -> 0 us
  Pallas kernels: 0 us -> 95.5 us
  blocking collectives: 24.5 us -> 0 us
  matrix products: 22.2 us -> 0 us
  other arithmetic: 16.5 us -> 0 us
  between operations: 14.3 us -> 0.64 us
  starting transfers between devices: 12.8 us -> 0 us
  local copies, waits for them, and re-layouts: 14.5 us -> 8.06 us
    reduce_scatter x1 -> x0, waiting for transfers between devices: 118 us -> none  [on_device(): lax.psum_scatter(terms_one, 'seq', scatter_dimension=0, tiled=True)]
    pallas_call x0 -> x1, Pallas kernels: none -> 95.5 us  [on_device(): pl.pallas_call(functools.partial(kernel, seq, spans, factor, reduce), out...]
    psum x1 -> x0, waiting for transfers between devices: 42.9 us -> none  [on_device(): first_weight_gradient = lax.psum(partial_rows, 'batch')]
    ppermute x4 -> x0, waiting for transfers between devices: 41.7 us -> none  [shifted(): lax.ppermute(value, axis, [(source, source + steps) for source in range(i...]
    all_to_all x1 -> x0, blocking collectives: 24.5 us -> none  [on_device(): lax.all_to_all(head_split_gradient, 'seq', split_axis=2, concat_axis=1, t...]
    dot_general x9 -> x0, matrix products: 22.2 us -> none  [the longest x2 6.43 us: input_grad(): jnp.einsum('co,sop->scp', weight[2], grad_lower, preferred_element_type=j...]
    ppermute x4 -> x0, starting transfers between devices: 12.7 us -> none  [shifted(): lax.ppermute(value, axis, [(source, source + steps) for source in range(i...]
    unnamed x1 -> x0, other arithmetic: 11.6 us -> none
  transfers between devices with their start and end apart: 6 -> 0, of which waited for: 4 -> 0; matrix products, arithmetic and copies ran while one was open for 7% -> 0% of each run, Pallas kernels for 0% -> 0%
where the time goes in v1:
time: 104 us
  Pallas kernels  95.5 us (92%)
  local copies, waits for them, and re-layouts  8.06 us (8%)
    pallas_call x1, Pallas kernels, on_device(): pl.pallas_call(functools.partial(kernel, seq, spans, factor, reduce), out...  95.5 us
    unnamed x2, local copies, waits for them, and re-layouts  4.86 us

profile of v1, /device:TPU:1, one launch (start us, length us, event | category | flops | bytes accessed | tf_op | source)
XLA Modules:
  0.0 104.2 jit_solution(13154060715174419301)
XLA Ops:
  0.6 1.6 %reshape.12.c1_ref = f32[768,1]{1,0:T(8,128)} reshape(f32[768]{0:T(1024)} %param.12) | data formatting | bytes 6144 | tf_op jit(solution)/shard_map/reshape | solution.py:415
  2.2 1.6 %reshape.13.c2_ref = f32[768,1]{1,0:T(8,128)} reshape(f32[768]{0:T(1024)} %param.13) | data formatting | bytes 6144 | tf_op jit(solution)/shard_map/reshape | solution.py:415
  3.8 95.5 %shard_map.86 = (bf16[768,512]{1,0:T(8,128)(2,1)}, f32[576,768]{1,0:T(8,128)}) custom-call(bf16[192,2048]{1,0:T(8,128)(2,1)} %bitcast.5, bf16[768,512]{1,0:T(8,128)(2,1)} %bitcast.6, bf16[768,512]{1,0:T(8,128)(2,1)} %bitcast.7, bf16[3,768,768]{2,1,0:T(8,128)(2,1)} %w1_hbm.1, bf16[3,768,768]{2,1,0:T(8,128)(2,1)} %w2_hbm.1, f32[768,1]{1,0:T(8,128)} %reshape.12.c1_ref, ...), custom_call_target="tpu_custom_call" | custom-call | flops 5435817984 | bytes 20000000 | tf_op jit(solution)/shard_map/pallas_call | solution.py:400
  99.3 2.1 %copy.13 = bf16[1,768,512]{2,1,0:T(8,128)(2,1)} copy(bf16[1,768,512]{2,1,0:T(8,128)(2,1)} %bitcast.4) | data formatting | bytes 1572864
  101.4 2.8 %copy.14 = f32[576,768]{1,0:T(8,128)} copy(f32[576,768]{1,0:T(8,128)} %get-tuple-element.9) | data formatting | bytes 3538944

commit v2 on v1

--- a/solution.py
+++ b/solution.py
@@ -38,7 +38,7 @@
     @pl.loop(0, chan // STRIP)
     def _(step):
         rows = pl.ds(pl.multiple_of(step * STRIP, STRIP), STRIP)
-        gain = gain_ref[rows, :]
+        gain = gain_ref[rows, 0:1]
         a = u_ref[rows, :].astype(F32) * scale * gain
         t = jnp.tanh(SLOPE * (a + CUBIC * a * a * a))
         slope = 0.5 * (1.0 + t) + 0.5 * a * (1.0 - t * t) * SLOPE * (1.0 + 3.0 * CUBIC * a * a)
@@ -86,10 +86,10 @@
 
 
 def kernel(
-    count, spans, factor, reduce,
+    count, spans, factor, early,
     h_ref, u1_ref, u2_ref, w1_hbm, w2_hbm, c1_ref, c2_ref,
     grad_ref, wgrad_ref,
-    w1, w2, e, m, slope1, slope2, scale1, scale2, gelu1, dg, terms,
+    gain1, gain2, w1, w2, e, m, slope1, slope2, scale1, scale2, gelu1, dg, terms,
     w_sem, a_send, a_recv, b_send, b_recv, *more,
 ):
     span_first, span_second = spans
@@ -106,7 +106,7 @@
     offsets = sorted(range(1, count), key=lambda j: -min(j, count - j))
     barrier = pltpu.get_barrier_semaphore()
     partners = [{"seq": lax.rem(z + j, count)} for j in offsets]
-    if reduce:
+    if early is not None:
         b = lax.axis_index("batch")
         x, core = b // 2, b % 2
         sib, across = x * 2 + 1 - core, (1 - x) * 2 + core
@@ -157,8 +157,10 @@
         else:
             pl.when(valid(side, z, span_second))(keep)
 
-    prepare(u2_ref, c2_ref, slope2, scale2, None)
-    prepare(u1_ref, c1_ref, slope1, scale1, gelu1)
+    for gain, row in ((gain1, c1_ref), (gain2, c2_ref)):
+        gain[...] = jnp.transpose(jnp.broadcast_to(row[...].reshape(1, chan), (gain.shape[1], chan)))
+    prepare(u2_ref, gain2, slope2, scale2, None)
+    prepare(u1_ref, gain1, slope1, scale1, gelu1)
     load2.wait()
 
     def border_copy(q, side):
@@ -218,6 +220,9 @@
             terms[pl.ds(tap * chan, chan), :] = jnp.zeros((chan, terms.shape[1]), F32)
 
     tap_terms(1, 1)
+    if early is not None:
+        reduction = Reduction(z, x, core, sib, across, early, terms, more)
+        reduction.start_early()
     border_terms(0, 2, sends_up)
     border_terms(2, 0, sends_down)
     load1.wait()
@@ -227,18 +232,18 @@
             grad_ref[rows, cols] = value
         return store
 
-    def first_layer():
+    def first_layer(q):
+        cols = pl.ds(q * piece, piece)
+        layer(
+            w1, m, sends_down, sends_up, cols,
+            u1_ref, slope1, scale1, dg, store_total(cols),
+        )
+
+    if early is not None:
+        reduction.run(first_layer, wgrad_ref)
+    else:
         for q in range(CHUNKS):
-            cols = pl.ds(q * piece, piece)
-            layer(
-                w1, m, sends_down, sends_up, cols,
-                u1_ref, slope1, scale1, dg, store_total(cols),
-            )
-
-    if reduce:
-        reduce_terms(count, z, x, core, sib, across, terms, wgrad_ref, first_layer, *more)
-    else:
-        first_layer()
+            first_layer(q)
         wgrad_ref[...] = terms[...]
 
     for q in range(CHUNKS):
@@ -253,98 +258,144 @@
             border_copy(q, 2).wait_send()
 
 
-def reduce_terms(
-    count, z, x, core, sib, across, terms, wgrad_ref, meanwhile,
-    core_out, core_in, x_out, x_in, z_out, z_in, kept, final,
-    core_send, core_recv, x_send, x_recv, z_send, z_recv, f_send, f_recv,
-):
-    rows_each, half = core_out.shape[1:]
-    order = sorted(range(count), key=lambda j: (j == 0, -min(j, count - j)))
-
-    def rows_of(j, part):
-        block = lax.rem(z + j, count)
-        return pl.ds(pl.multiple_of(block * (2 * rows_each) + part * rows_each, 16), rows_each)
-
-    mine = pl.ds(pl.multiple_of(core * half, 128), half)
-    theirs = pl.ds(pl.multiple_of((1 - core) * half, 128), half)
-
-    def core_copy(slot):
+class Reduction:
+    def __init__(self, z, x, core, sib, across, early, terms, refs):
+        self.z, self.x, self.core, self.sib, self.across = z, x, core, sib, across
+        self.terms = terms
+        (self.core_out, self.core_in, self.x_out, self.x_in, self.z_out, self.z_in, self.kept,
+         self.core_send, self.core_recv, self.x_send, self.x_recv,
+         self.z_send, self.z_recv, self.f_send, self.f_recv) = refs
+        self.each, self.half = self.core_out.shape[1:]
+        self.mine = pl.ds(pl.multiple_of(core * self.half, 128), self.half)
+        self.theirs = pl.ds(pl.multiple_of((1 - core) * self.half, 128), self.half)
+        self.early_block = early[1] + x * (early[0] - early[1])
+        self.early_unit = flip(self.early_block, z % 2, z // 2)
+
+    def block(self, k):
+        return flip(self.z, k % 2, k // 2)
+
+    def rows(self, block, part):
+        return pl.ds(pl.multiple_of((block * 2 + part) * self.each, 16), self.each)
+
+    def core_copy(self, slot):
         return pltpu.make_async_remote_copy(
-            src_ref=core_out.at[slot], dst_ref=core_in.at[slot],
-            send_sem=core_send.at[slot], recv_sem=core_recv.at[slot],
-            device_id={"batch": sib}, device_id_type=MESH,
-        )
-
-    def x_copy(j):
+            src_ref=self.core_out.at[slot], dst_ref=self.core_in.at[slot],
+            send_sem=self.core_send.at[slot], recv_sem=self.core_recv.at[slot],
+            device_id={"batch": self.sib}, device_id_type=MESH,
+        )
+
+    def x_copy(self, k):
         return pltpu.make_async_remote_copy(
-            src_ref=x_out.at[j], dst_ref=x_in.at[j],
-            send_sem=x_send.at[j], recv_sem=x_recv.at[j],
-            device_id={"batch": across}, device_id_type=MESH,
-        )
-
-    def z_copy(j, dest):
+            src_ref=self.x_out.at[k], dst_ref=self.x_in.at[k],
+            send_sem=self.x_send.at[k], recv_sem=self.x_recv.at[k],
+            device_id={"batch": self.across}, device_id_type=MESH,
+        )
+
+    def z_copy(self, slot):
         return pltpu.make_async_remote_copy(
-            src_ref=z_out.at[j - 1], dst_ref=z_in.at[j - 1],
-            send_sem=z_send.at[j - 1], recv_sem=z_recv.at[j - 1],
-            device_id={"seq": dest}, device_id_type=MESH,
-        )
-
-    for group, part in ((0, 1 - x), (1, x)):
-        for j in order:
-            slot = group * count + j
-            core_out[slot] = terms[rows_of(j, part), theirs].astype(BF16)
-            core_copy(slot).start()
-    for j in order:
-        core_copy(j).wait_recv()
-        x_out[j] = (terms[rows_of(j, 1 - x), mine] + core_in[j].astype(F32)).astype(BF16)
-        x_copy(j).start()
-
-    meanwhile()
-
-    for j in order:
-        core_copy(count + j).wait_recv()
-        x_copy(j).wait_recv()
-        total = terms[rows_of(j, x), mine] + core_in[count + j].astype(F32) + x_in[j].astype(F32)
-        if j == 0:
-            kept[...] = total
-        else:
-            z_out[j - 1] = total.astype(BF16)
-            z_copy(j, lax.rem(z + j, count)).start()
-    for j in order[:-1]:
-        z_copy(j, lax.rem(z + j, count)).wait_recv()
-        kept[...] += z_in[j - 1].astype(F32)
-
-    me = x * 2 + core
-    final[me] = kept[...].astype(BF16)
-
-    def final_copy(index, slot, to):
-        return pltpu.make_async_remote_copy(
-            src_ref=final.at[slot], dst_ref=final.at[slot],
-            send_sem=f_send.at[index], recv_sem=f_recv.at[index],
-            device_id={"batch": to}, device_id_type=MESH,
-        )
-
-    final_copy(0, me, across).start()
-    final_copy(1, me, sib).start()
-    final_copy(0, across, across).wait_recv()
-    final_copy(2, across, sib).start()
-    final_copy(1, sib, sib).wait_recv()
-    final_copy(2, (1 - x) * 2 + 1 - core, sib).wait_recv()
+            src_ref=self.z_out.at[slot], dst_ref=self.z_in.at[slot],
+            send_sem=self.z_send.at[slot], recv_sem=self.z_recv.at[slot],
+            device_id={"seq": self.block(2 if slot == 2 else 1)}, device_id_type=MESH,
+        )
+
+    def to_core(self, slot, block, part):
+        self.core_out[slot] = self.terms[self.rows(block, part), self.theirs].astype(BF16)
+        self.core_copy(slot).start()
+
+    def to_x(self, k, block):
+        self.core_copy(k).wait_recv()
+        own = self.terms[self.rows(block, 1 - self.x), self.mine]
+        self.x_out[k] = (own + self.core_in[k].astype(F32)).astype(BF16)
+        self.x_copy(k).start()
+
+    def start_early(self):
+        self.to_core(self.early_unit, self.early_block, 1 - self.x)
+        self.to_x(self.early_unit, self.early_block)
+
+    def run(self, meanwhile, final):
+        for k in (3, 2, 1, 0):
+            @pl.when(k != self.early_unit)
+            def _():
+                self.to_core(k, self.block(k), 1 - self.x)
+        for k in (3, 2, 1, 0):
+            self.to_core(4 + k, self.block(k), self.x)
+        for k in (3, 2, 1, 0):
+            @pl.when(k != self.early_unit)
+            def _():
+                self.to_x(k, self.block(k))
+        meanwhile(0)
+        for k in (3, 2, 1, 0):
+            self.core_copy(4 + k).wait_recv()
+            self.x_copy(k).wait_recv()
+            own = self.terms[self.rows(self.block(k), self.x), self.mine]
+            total = own + self.core_in[4 + k].astype(F32) + self.x_in[k].astype(F32)
+            if k == 2:
+                self.z_copy(0).wait_recv()
+                total = total + self.z_in[0].astype(F32)
+            if k == 0:
+                self.kept[...] = total
+            else:
+                slot = {3: 0, 1: 1, 2: 2}[k]
+                self.z_out[slot] = total.astype(BF16)
+                self.z_copy(slot).start()
+            if k == 3:
+                meanwhile(1)
+        self.z_copy(1).wait_recv()
+        self.kept[...] += self.z_in[1].astype(F32)
+        self.z_copy(2).wait_recv()
+        me = self.x * 2 + self.core
+        final[me] = (self.kept[...] + self.z_in[2].astype(F32)).astype(BF16)
+
+        def final_copy(index, slot, to):
+            return pltpu.make_async_remote_copy(
+                src_ref=final.at[slot], dst_ref=final.at[slot],
+                send_sem=self.f_send.at[index], recv_sem=self.f_recv.at[index],
+                device_id={"batch": to}, device_id_type=MESH,
+            )
+
+        sib, across = self.sib, self.across
+        final_copy(0, me, across).start()
+        final_copy(1, me, sib).start()
+        final_copy(0, across, across).wait_recv()
+        final_copy(2, across, sib).start()
+        final_copy(1, sib, sib).wait_recv()
+        final_copy(2, (1 - self.x) * 2 + 1 - self.core, sib).wait_recv()
+
+        final_copy(0, me, across).wait_send()
+        final_copy(1, me, sib).wait_send()
+        final_copy(2, across, sib).wait_send()
+        for slot in range(8):
+            self.core_copy(slot).wait_send()
+        for k in range(4):
+            self.x_copy(k).wait_send()
+        for slot in range(3):
+            self.z_copy(slot).wait_send()
+
+
+def flip(value, bit, high):
+    low_part, high_part = value % 2, value // 2
+    return 2 * (high_part + high - 2 * high_part * high) + low_part + bit - 2 * low_part * bit
+
+
+def finish(grad_hbm, parts_hbm, grad_out, wgrad_out, grad, parts, wgrad, sems):
+    each, half = parts.shape[1:]
+    into = pltpu.make_async_copy(grad_hbm, grad, sems.at[0])
+    parts_in = pltpu.make_async_copy(parts_hbm, parts, sems.at[1])
+    parts_in.start()
+    into.start()
+    parts_in.wait()
+    out = []
     for part in range(2):
+        rows = pl.ds(part * each, each)
         for side in range(2):
-            wgrad_ref[pl.ds(part * rows_each, rows_each), pl.ds(side * half, half)] = final[
-                part * 2 + side
-            ].astype(F32)
-
-    final_copy(0, me, across).wait_send()
-    final_copy(1, me, sib).wait_send()
-    final_copy(2, across, sib).wait_send()
-    for slot in range(2 * count):
-        core_copy(slot).wait_send()
-    for j in range(count):
-        x_copy(j).wait_send()
-    for j in range(1, count):
-        z_copy(j, lax.rem(z + j, count)).wait_send()
+            wgrad[rows, pl.ds(side * half, half)] = parts[part * 2 + side].astype(F32)
+        out.append(pltpu.make_async_copy(wgrad.at[rows], wgrad_out.at[rows], sems.at[3 + part]))
+        out[-1].start()
+    into.wait()
+    out.append(pltpu.make_async_copy(grad, grad_out, sems.at[2]))
+    out[-1].start()
+    for copy in out:
+        copy.wait()
 
 
 def on_device(seq, batch, head, u1, u2, w1, w2, c1, c2):
@@ -355,12 +406,24 @@
     factor = 1.0 / math.sqrt(u1.shape[0] * batch * width * seq)
     spans = (DILATION_FIRST // width, DILATION_SECOND // width)
     rows = total_rows // seq
-    reduce = batch == 4 and rows % 32 == 0 and out_chan % 256 == 0
     rows_each, half = rows // 2, out_chan // 2
+    early = [
+        [
+            block for block in range(seq)
+            if chan <= (2 * block + part) * rows_each <= 2 * chan - rows_each
+        ][:1]
+        for part in range(2)
+    ]
+    reduce = (
+        seq == 4 and batch == 4 and rows % 32 == 0 and out_chan % 256 == 0 and all(early)
+    )
+    early = [blocks[0] for blocks in early] if reduce else None
     vmem = pl.BlockSpec(memory_space=pltpu.VMEM)
     anywhere = pl.BlockSpec(memory_space=pl.ANY)
     dma = pltpu.SemaphoreType.DMA
     scratch = [
+        pltpu.VMEM((chan, 128), F32),
+        pltpu.VMEM((chan, 128), F32),
         pltpu.VMEM(w1.shape, BF16),
         pltpu.VMEM(w2.shape, BF16),
         pltpu.VMEM((3, chan, width), BF16),
@@ -387,7 +450,6 @@
             pltpu.VMEM((seq - 1, rows_each, half), BF16),
             pltpu.VMEM((seq - 1, rows_each, half), BF16),
             pltpu.VMEM((rows_each, half), F32),
-            pltpu.VMEM((4, rows_each, half), BF16),
             dma((2 * seq,)),
             dma((2 * seq,)),
             dma((seq,)),
@@ -398,10 +460,11 @@
             dma((3,)),
         ]
     grad, wgrad = pl.pallas_call(
-        functools.partial(kernel, seq, spans, factor, reduce),
+        functools.partial(kernel, seq, spans, factor, early),
         out_shape=(
             jax.ShapeDtypeStruct((chan, width), BF16),
-            jax.ShapeDtypeStruct((rows if reduce else total_rows, out_chan), F32),
+            jax.ShapeDtypeStruct((4, rows_each, half), BF16)
+            if reduce else jax.ShapeDtypeStruct((total_rows, out_chan), F32),
         ),
         in_specs=[vmem, vmem, vmem, anywhere, anywhere, vmem, vmem],
         out_specs=(vmem, vmem),
@@ -412,8 +475,26 @@
         cost_estimate=pl.CostEstimate(
             flops=18 * chan * out_chan * width, bytes_accessed=20_000_000, transcendentals=2 * chan * width
         ),
-    )(head[0], u1[0], u2[0], w1, w2, c1.reshape(chan, 1), c2.reshape(chan, 1))
-    if not reduce:
+    )(head[0], u1[0], u2[0], w1, w2, c1, c2)
+    if reduce:
+        shapes = (
+            jax.ShapeDtypeStruct(grad.shape, BF16),
+            jax.ShapeDtypeStruct((rows, out_chan), F32),
+        )
+        grad, wgrad = pl.pallas_call(
+            finish,
+            out_shape=shapes,
+            in_specs=[anywhere, anywhere],
+            out_specs=(anywhere, anywhere),
+            scratch_shapes=[
+                pltpu.VMEM(grad.shape, BF16),
+                pltpu.VMEM(wgrad.shape, BF16),
+                pltpu.VMEM((rows, out_chan), F32),
+                dma((5,)),
+            ],
+            compiler_params=pltpu.CompilerParams(vmem_limit_bytes=56 * 1024 * 1024),
+        )(grad, wgrad)
+    else:
         wgrad = lax.psum(lax.psum_scatter(wgrad, "seq", scatter_dimension=0, tiled=True), "batch")
     return grad[None], wgrad
 

time: 104 us -> 100 us (0.962)
  local copies, waits for them, and re-layouts: 8.06 us -> 0 us
  Pallas kernels: 95.5 us -> 99.4 us
    unnamed x2 -> x0, local copies, waits for them, and re-layouts: 4.86 us -> none
    pallas_call x1 -> x2, Pallas kernels: 95.5 us -> 99.4 us  [the longest x1 96.6 us: on_device(): pl.pallas_call(functools.partial(kernel, seq, spans, factor, early), out_...]
    reshape x2 -> x0, local copies, waits for them, and re-layouts: 3.2 us -> none  [the longest x1 1.6 us: on_device(): c1.reshape(chan, 1)]
where the time goes in v2:
time: 100 us
  Pallas kernels  99.4 us (99%)
    pallas_call x1, Pallas kernels, on_device(): pl.pallas_call(functools.partial(kernel, seq, spans, factor, early), out_...  96.6 us
    pallas_call x1, Pallas kernels, on_device(): pl.pallas_call(finish, out_shape=shapes, in_specs=[anywhere, anywhere], o...  2.73 us

profile of v2, /device:TPU:1, one launch (start us, length us, event | category | flops | bytes accessed | tf_op | source)
XLA Modules:
  0.0 100.0 jit_solution(9909665178791628541)
XLA Ops:
  0.6 96.6 %shard_map.86 = (bf16[768,512]{1,0:T(8,128)(2,1)}, bf16[4,288,384]{2,1,0:T(8,128)(2,1)}) custom-call(bf16[192,2048]{1,0:T(8,128)(2,1)} %bitcast.4, bf16[768,512]{1,0:T(8,128)(2,1)} %bitcast.5, bf16[768,512]{1,0:T(8,128)(2,1)} %bitcast.6, bf16[3,768,768]{2,1,0:T(8,128)(2,1)} %w1_hbm.1, bf16[3,768,768]{2,1,0:T(8,128)(2,1)} %w2_hbm.1, f32[768]{0:T(1024)} %c1_ref.1, ...), custom_call_target="tpu_custom_call" | custom-call | flops 5435817984 | bytes 20000000 | tf_op jit(solution)/shard_map/pallas_call | solution.py:462
  97.3 2.7 %shard_map.87 = (bf16[768,512]{1,0:T(8,128)(2,1)}, f32[576,768]{1,0:T(8,128)}) custom-call(bf16[768,512]{1,0:T(8,128)(2,1)} %get-tuple-element.6.grad_hbm, bf16[4,288,384]{2,1,0:T(8,128)(2,1)} %get-tuple-element.7.parts_hbm), custom_call_target="tpu_custom_call" | custom-call | tf_op jit(solution)/shard_map/pallas_call | solution.py:484

commit v3 on v2

--- a/solution.py
+++ b/solution.py
@@ -20,7 +20,7 @@
 MESH = pl.DeviceIdType.MESH
 CHUNKS = 2
 STRIP = 64
-BLOCK = 256
+BLOCK = 768
 
 
 def prepare(u_ref, gain_ref, slope_ref, scale_ref, gelu_ref):
@@ -87,9 +87,9 @@
 
 def kernel(
     count, spans, factor, early,
-    h_ref, u1_ref, u2_ref, w1_hbm, w2_hbm, c1_ref, c2_ref,
-    grad_ref, wgrad_ref,
-    gain1, gain2, w1, w2, e, m, slope1, slope2, scale1, scale2, gelu1, dg, terms,
+    h_ref, u1_hbm, u2_hbm, w1_hbm, w2_hbm, c1_ref, c2_ref,
+    grad_hbm, wgrad_hbm,
+    u1_ref, u2_ref, grad_ref, gain1, gain2, w1, w2, e, m, slope1, slope2, scale1, scale2, gelu1, dg, terms,
     w_sem, a_send, a_recv, b_send, b_recv, *more,
 ):
     span_first, span_second = spans
@@ -100,8 +100,8 @@
 
     load2 = pltpu.make_async_copy(w2_hbm, w2, w_sem.at[0])
     load1 = pltpu.make_async_copy(w1_hbm, w1, w_sem.at[1])
-    load2.start()
-    load1.start()
+    load_u2 = pltpu.make_async_copy(u2_hbm, u2_ref, w_sem.at[2])
+    load_u1 = pltpu.make_async_copy(u1_hbm, u1_ref, w_sem.at[3])
 
     offsets = sorted(range(1, count), key=lambda j: -min(j, count - j))
     barrier = pltpu.get_barrier_semaphore()
@@ -148,20 +148,32 @@
         each_share(q, lambda copy: copy.start(), False)
 
     own = pl.ds(pl.multiple_of(z * share, 16), share)
-    for side in (0, 1, 2):
-        def keep(side=side):
-            at = pl.multiple_of((z + (side - 1) * span_second) * width, 128)
-            e[side, own, :] = h_ref[:, pl.ds(at, width)]
-        if side == 1:
-            keep()
-        else:
-            pl.when(valid(side, z, span_second))(keep)
-
+
+    def each_own(act):
+        for side in (0, 1, 2):
+            def keep(side=side):
+                at = pl.multiple_of((z + (side - 1) * span_second) * width, 128)
+                act(pltpu.make_async_copy(
+                    h_ref.at[:, pl.ds(at, width)], e.at[side, own, :], w_sem.at[4 + side]
+                ))
+            if side == 1:
+                keep()
+            else:
+                pl.when(valid(side, z, span_second))(keep)
+
+    load_u2.start()
+    load_u1.start()
+    each_own(lambda copy: copy.start())
+    load2.start()
+    load1.start()
     for gain, row in ((gain1, c1_ref), (gain2, c2_ref)):
         gain[...] = jnp.transpose(jnp.broadcast_to(row[...].reshape(1, chan), (gain.shape[1], chan)))
+    load_u2.wait()
     prepare(u2_ref, gain2, slope2, scale2, None)
+    load_u1.wait()
     prepare(u1_ref, gain1, slope1, scale1, gelu1)
     load2.wait()
+    each_own(lambda copy: copy.wait())
 
     def border_copy(q, side):
         to = z + span_first if side == 0 else z - span_first
@@ -232,19 +244,28 @@
             grad_ref[rows, cols] = value
         return store
 
+    def result_copy(q):
+        cols = pl.ds(q * piece, piece)
+        return pltpu.make_async_copy(grad_ref.at[:, cols], grad_hbm.at[:, cols], w_sem.at[7 + q])
+
     def first_layer(q):
         cols = pl.ds(q * piece, piece)
         layer(
             w1, m, sends_down, sends_up, cols,
             u1_ref, slope1, scale1, dg, store_total(cols),
         )
+        result_copy(q).start()
 
     if early is not None:
-        reduction.run(first_layer, wgrad_ref)
+        reduction.run(first_layer, wgrad_hbm)
     else:
         for q in range(CHUNKS):
             first_layer(q)
-        wgrad_ref[...] = terms[...]
+        terms_out = pltpu.make_async_copy(terms, wgrad_hbm, w_sem.at[0])
+        terms_out.start()
+        terms_out.wait()
+    for q in range(CHUNKS):
+        result_copy(q).wait()
 
     for q in range(CHUNKS):
         each_share(q, lambda copy: copy.wait_send(), False)
@@ -262,9 +283,9 @@
     def __init__(self, z, x, core, sib, across, early, terms, refs):
         self.z, self.x, self.core, self.sib, self.across = z, x, core, sib, across
         self.terms = terms
-        (self.core_out, self.core_in, self.x_out, self.x_in, self.z_out, self.z_in, self.kept,
+        (self.core_out, self.core_in, self.x_out, self.x_in, self.z_out, self.z_in, self.kept, self.final,
          self.core_send, self.core_recv, self.x_send, self.x_recv,
-         self.z_send, self.z_recv, self.f_send, self.f_recv) = refs
+         self.z_send, self.z_recv, self.f_send, self.f_recv, self.o_sem) = refs
         self.each, self.half = self.core_out.shape[1:]
         self.mine = pl.ds(pl.multiple_of(core * self.half, 128), self.half)
         self.theirs = pl.ds(pl.multiple_of((1 - core) * self.half, 128), self.half)
@@ -312,7 +333,8 @@
         self.to_core(self.early_unit, self.early_block, 1 - self.x)
         self.to_x(self.early_unit, self.early_block)
 
-    def run(self, meanwhile, final):
+    def run(self, meanwhile, wgrad_hbm):
+        final = self.final
         for k in (3, 2, 1, 0):
             @pl.when(k != self.early_unit)
             def _():
@@ -356,10 +378,19 @@
         sib, across = self.sib, self.across
         final_copy(0, me, across).start()
         final_copy(1, me, sib).start()
+        last = (1 - self.x) * 2 + 1 - self.core
+
+        def out_copy(slot):
+            return pltpu.make_async_copy(final.at[slot], wgrad_hbm.at[slot], self.o_sem.at[slot])
+
+        out_copy(me).start()
+        final_copy(1, sib, sib).wait_recv()
+        out_copy(sib).start()
         final_copy(0, across, across).wait_recv()
         final_copy(2, across, sib).start()
-        final_copy(1, sib, sib).wait_recv()
-        final_copy(2, (1 - self.x) * 2 + 1 - self.core, sib).wait_recv()
+        out_copy(across).start()
+        final_copy(2, last, sib).wait_recv()
+        out_copy(last).start()
 
         final_copy(0, me, across).wait_send()
         final_copy(1, me, sib).wait_send()
@@ -370,6 +401,8 @@
             self.x_copy(k).wait_send()
         for slot in range(3):
             self.z_copy(slot).wait_send()
+        for slot in range(4):
+            out_copy(slot).wait()
 
 
 def flip(value, bit, high):
@@ -422,6 +455,9 @@
     anywhere = pl.BlockSpec(memory_space=pl.ANY)
     dma = pltpu.SemaphoreType.DMA
     scratch = [
+        pltpu.VMEM((chan, width), BF16),
+        pltpu.VMEM((chan, width), BF16),
+        pltpu.VMEM((chan, width), BF16),
         pltpu.VMEM((chan, 128), F32),
         pltpu.VMEM((chan, 128), F32),
         pltpu.VMEM(w1.shape, BF16),
@@ -435,7 +471,7 @@
         pltpu.VMEM((chan, width), BF16),
         pltpu.VMEM((chan, width // CHUNKS), F32),
         pltpu.VMEM((total_rows, out_chan), F32),
-        dma((2,)),
+        dma((7 + CHUNKS,)),
         dma((CHUNKS, seq - 1, 3)),
         dma((CHUNKS, seq - 1, 3)),
         dma((CHUNKS, 2)),
@@ -450,6 +486,7 @@
             pltpu.VMEM((seq - 1, rows_each, half), BF16),
             pltpu.VMEM((seq - 1, rows_each, half), BF16),
             pltpu.VMEM((rows_each, half), F32),
+            pltpu.VMEM((4, rows_each, half), BF16),
             dma((2 * seq,)),
             dma((2 * seq,)),
             dma((seq,)),
@@ -458,6 +495,7 @@
             dma((seq - 1,)),
             dma((3,)),
             dma((3,)),
+            dma((4,)),
         ]
     grad, wgrad = pl.pallas_call(
         functools.partial(kernel, seq, spans, factor, early),
@@ -466,8 +504,8 @@
             jax.ShapeDtypeStruct((4, rows_each, half), BF16)
             if reduce else jax.ShapeDtypeStruct((total_rows, out_chan), F32),
         ),
-        in_specs=[vmem, vmem, vmem, anywhere, anywhere, vmem, vmem],
-        out_specs=(vmem, vmem),
+        in_specs=[anywhere] * 5 + [vmem, vmem],
+        out_specs=(anywhere, anywhere),
         scratch_shapes=scratch,
         compiler_params=pltpu.CompilerParams(
             collective_id=0, has_side_effects=True, vmem_limit_bytes=56 * 1024 * 1024

time: 100 us -> 99 us (0.990)
  Pallas kernels: 99.4 us -> 98.1 us
    pallas_call x1, Pallas kernels: 96.6 us -> 95.4 us  [on_device(): pl.pallas_call(functools.partial(kernel, seq, spans, factor, early), out_...]
where the time goes in v3:
time: 99 us; the launch traced here: 98.8 us
  Pallas kernels  98.1 us (99%)
    pallas_call x1, Pallas kernels, on_device(): pl.pallas_call(functools.partial(kernel, seq, spans, factor, early), out_...  95.4 us
    pallas_call x1, Pallas kernels, on_device(): pl.pallas_call(finish, out_shape=shapes, in_specs=[anywhere, anywhere], o...  2.73 us

profile of v3, /device:TPU:1, one launch (start us, length us, event | category | flops | bytes accessed | tf_op | source)
XLA Modules:
  0.0 98.8 jit_solution(2106078770892920454)
XLA Ops:
  0.6 95.4 %shard_map.86 = (bf16[768,512]{1,0:T(8,128)(2,1)}, bf16[4,288,384]{2,1,0:T(8,128)(2,1)}) custom-call(bf16[192,2048]{1,0:T(8,128)(2,1)} %bitcast.4, bf16[768,512]{1,0:T(8,128)(2,1)} %bitcast.5, bf16[768,512]{1,0:T(8,128)(2,1)} %bitcast.6, bf16[3,768,768]{2,1,0:T(8,128)(2,1)} %w1_hbm.1, bf16[3,768,768]{2,1,0:T(8,128)(2,1)} %w2_hbm.1, f32[768]{0:T(1024)} %c1_ref.1, ...), custom_call_target="tpu_custom_call" | custom-call | flops 5435817984 | bytes 20000000 | tf_op jit(solution)/shard_map/pallas_call | solution.py:500
  96.0 2.7 %shard_map.87 = (bf16[768,512]{1,0:T(8,128)(2,1)}, f32[576,768]{1,0:T(8,128)}) custom-call(bf16[768,512]{1,0:T(8,128)(2,1)} %get-tuple-element.6.grad_hbm, bf16[4,288,384]{2,1,0:T(8,128)(2,1)} %get-tuple-element.7.parts_hbm), custom_call_target="tpu_custom_call" | custom-call | tf_op jit(solution)/shard_map/pallas_call | solution.py:522

commit v4 on v3

--- a/solution.py
+++ b/solution.py
@@ -18,7 +18,7 @@
 F32 = jnp.float32
 BF16 = jnp.bfloat16
 MESH = pl.DeviceIdType.MESH
-CHUNKS = 2
+CHUNKS = 4
 STRIP = 64
 BLOCK = 768
 
@@ -257,7 +257,11 @@
         result_copy(q).start()
 
     if early is not None:
-        reduction.run(first_layer, wgrad_hbm)
+        def first_layer_part(part):
+            for q in range(part * CHUNKS // 2, (part + 1) * CHUNKS // 2):
+                first_layer(q)
+
+        reduction.run(first_layer_part, wgrad_hbm)
     else:
         for q in range(CHUNKS):
             first_layer(q)
@@ -295,8 +299,8 @@
     def block(self, k):
         return flip(self.z, k % 2, k // 2)
 
-    def rows(self, block, part):
-        return pl.ds(pl.multiple_of((block * 2 + part) * self.each, 16), self.each)
+    def rows(self, turn, block, part):
+        return pl.ds(pl.multiple_of(((block * 2 + part) * 2 + turn) * self.each, 16), self.each)
 
     def core_copy(self, slot):
         return pltpu.make_async_remote_copy(
@@ -312,95 +316,127 @@
             device_id={"batch": self.across}, device_id_type=MESH,
         )
 
-    def z_copy(self, slot):
+    def z_copy(self, turn, kind):
+        slot = turn * 3 + kind
         return pltpu.make_async_remote_copy(
             src_ref=self.z_out.at[slot], dst_ref=self.z_in.at[slot],
             send_sem=self.z_send.at[slot], recv_sem=self.z_recv.at[slot],
-            device_id={"seq": self.block(2 if slot == 2 else 1)}, device_id_type=MESH,
-        )
-
-    def to_core(self, slot, block, part):
-        self.core_out[slot] = self.terms[self.rows(block, part), self.theirs].astype(BF16)
-        self.core_copy(slot).start()
-
-    def to_x(self, k, block):
-        self.core_copy(k).wait_recv()
-        own = self.terms[self.rows(block, 1 - self.x), self.mine]
-        self.x_out[k] = (own + self.core_in[k].astype(F32)).astype(BF16)
-        self.x_copy(k).start()
+            device_id={"seq": self.block(2 if kind == 2 else 1)}, device_id_type=MESH,
+        )
+
+    def to_core(self, turn, slot, block, part):
+        self.core_out[turn * 8 + slot] = self.terms[
+            self.rows(turn, block, part), self.theirs
+        ].astype(BF16)
+        self.core_copy(turn * 8 + slot).start()
+
+    def to_x(self, turn, k, block):
+        self.core_copy(turn * 8 + k).wait_recv()
+        own = self.terms[self.rows(turn, block, 1 - self.x), self.mine]
+        total = own + self.core_in[turn * 8 + k].astype(F32)
+        self.x_out[turn * 4 + k] = total.astype(BF16)
+        self.x_copy(turn * 4 + k).start()
 
     def start_early(self):
-        self.to_core(self.early_unit, self.early_block, 1 - self.x)
-        self.to_x(self.early_unit, self.early_block)
+        for turn in range(2):
+            self.to_core(turn, self.early_unit, self.early_block, 1 - self.x)
+        for turn in range(2):
+            self.to_x(turn, self.early_unit, self.early_block)
+
+    def stage(self, turn, k):
+        self.core_copy(turn * 8 + 4 + k).wait_recv()
+        self.x_copy(turn * 4 + k).wait_recv()
+        own = self.terms[self.rows(turn, self.block(k), self.x), self.mine]
+        total = own + self.core_in[turn * 8 + 4 + k].astype(F32)
+        total = total + self.x_in[turn * 4 + k].astype(F32)
+        if k == 2:
+            self.z_copy(turn, 0).wait_recv()
+            total = total + self.z_in[turn * 3].astype(F32)
+        if k == 0:
+            self.kept[turn] = total
+        else:
+            kind = {3: 0, 1: 1, 2: 2}[k]
+            self.z_out[turn * 3 + kind] = total.astype(BF16)
+            self.z_copy(turn, kind).start()
+
+    def final_copy(self, turn, index, slot, to):
+        place = self.final.at[slot, pl.ds(turn * self.each, self.each)]
+        return pltpu.make_async_remote_copy(
+            src_ref=place, dst_ref=place,
+            send_sem=self.f_send.at[turn, index], recv_sem=self.f_recv.at[turn, index],
+            device_id={"batch": to}, device_id_type=MESH,
+        )
+
+    def gather(self, turn):
+        self.z_copy(turn, 1).wait_recv()
+        total = self.kept[turn] + self.z_in[turn * 3 + 1].astype(F32)
+        self.z_copy(turn, 2).wait_recv()
+        total = total + self.z_in[turn * 3 + 2].astype(F32)
+        me = self.x * 2 + self.core
+        self.final[me, pl.ds(turn * self.each, self.each)] = total.astype(BF16)
+        self.final_copy(turn, 0, me, self.across).start()
+        self.final_copy(turn, 1, me, self.sib).start()
+
+    def forward(self, turn):
+        self.final_copy(turn, 0, self.across, self.across).wait_recv()
+        self.final_copy(turn, 2, self.across, self.sib).start()
 
     def run(self, meanwhile, wgrad_hbm):
-        final = self.final
-        for k in (3, 2, 1, 0):
-            @pl.when(k != self.early_unit)
-            def _():
-                self.to_core(k, self.block(k), 1 - self.x)
-        for k in (3, 2, 1, 0):
-            self.to_core(4 + k, self.block(k), self.x)
-        for k in (3, 2, 1, 0):
-            @pl.when(k != self.early_unit)
-            def _():
-                self.to_x(k, self.block(k))
+        units = (3, 2, 1, 0)
+        for turn in range(2):
+            for k in units:
+                @pl.when(k != self.early_unit)
+                def _():
+                    self.to_core(turn, k, self.block(k), 1 - self.x)
+        for turn in range(2):
+            for k in units:
+                @pl.when(k != self.early_unit)
+                def _():
+                    self.to_x(turn, k, self.block(k))
+            for k in units:
+                self.to_core(turn, 4 + k, self.block(k), self.x)
         meanwhile(0)
-        for k in (3, 2, 1, 0):
-            self.core_copy(4 + k).wait_recv()
-            self.x_copy(k).wait_recv()
-            own = self.terms[self.rows(self.block(k), self.x), self.mine]
-            total = own + self.core_in[4 + k].astype(F32) + self.x_in[k].astype(F32)
-            if k == 2:
-                self.z_copy(0).wait_recv()
-                total = total + self.z_in[0].astype(F32)
-            if k == 0:
-                self.kept[...] = total
-            else:
-                slot = {3: 0, 1: 1, 2: 2}[k]
-                self.z_out[slot] = total.astype(BF16)
-                self.z_copy(slot).start()
-            if k == 3:
-                meanwhile(1)
-        self.z_copy(1).wait_recv()
-        self.kept[...] += self.z_in[1].astype(F32)
-        self.z_copy(2).wait_recv()
-        me = self.x * 2 + self.core
-        final[me] = (self.kept[...] + self.z_in[2].astype(F32)).astype(BF16)
-
-        def final_copy(index, slot, to):
-            return pltpu.make_async_remote_copy(
-                src_ref=final.at[slot], dst_ref=final.at[slot],
-                send_sem=self.f_send.at[index], recv_sem=self.f_recv.at[index],
-                device_id={"batch": to}, device_id_type=MESH,
+        self.stage(0, 3)
+        self.stage(0, 2)
+        meanwhile(1)
+        self.stage(0, 1)
+        self.stage(0, 0)
+        self.stage(1, 3)
+        self.stage(1, 2)
+        self.gather(0)
+        self.stage(1, 1)
+        self.stage(1, 0)
+        self.forward(0)
+        self.gather(1)
+
+        me, sib, across = self.x * 2 + self.core, self.sib, self.across
+        last = (1 - self.x) * 2 + 1 - self.core
+
+        def out_copy(slot):
+            return pltpu.make_async_copy(
+                self.final.at[slot], wgrad_hbm.at[slot], self.o_sem.at[slot]
             )
 
-        sib, across = self.sib, self.across
-        final_copy(0, me, across).start()
-        final_copy(1, me, sib).start()
-        last = (1 - self.x) * 2 + 1 - self.core
-
-        def out_copy(slot):
-            return pltpu.make_async_copy(final.at[slot], wgrad_hbm.at[slot], self.o_sem.at[slot])
-
         out_copy(me).start()
-        final_copy(1, sib, sib).wait_recv()
+        for turn in range(2):
+            self.final_copy(turn, 1, sib, sib).wait_recv()
         out_copy(sib).start()
-        final_copy(0, across, across).wait_recv()
-        final_copy(2, across, sib).start()
+        self.forward(1)
         out_copy(across).start()
-        final_copy(2, last, sib).wait_recv()
+        for turn in range(2):
+            self.final_copy(turn, 2, last, sib).wait_recv()
         out_copy(last).start()
 
-        final_copy(0, me, across).wait_send()
-        final_copy(1, me, sib).wait_send()
-        final_copy(2, across, sib).wait_send()
-        for slot in range(8):
+        for turn in range(2):
+            self.final_copy(turn, 0, me, across).wait_send()
+            self.final_copy(turn, 1, me, sib).wait_send()
+            self.final_copy(turn, 2, across, sib).wait_send()
+            for kind in range(3):
+                self.z_copy(turn, kind).wait_send()
+        for slot in range(16):
             self.core_copy(slot).wait_send()
-        for k in range(4):
+        for k in range(8):
             self.x_copy(k).wait_send()
-        for slot in range(3):
-            self.z_copy(slot).wait_send()
         for slot in range(4):
             out_copy(slot).wait()
 
@@ -448,7 +484,7 @@
         for part in range(2)
     ]
     reduce = (
-        seq == 4 and batch == 4 and rows % 32 == 0 and out_chan % 256 == 0 and all(early)
+        seq == 4 and batch == 4 and rows % 64 == 0 and out_chan % 256 == 0 and all(early)
     )
     early = [blocks[0] for blocks in early] if reduce else None
     vmem = pl.BlockSpec(memory_space=pltpu.VMEM)
@@ -478,23 +514,24 @@
         dma((CHUNKS, 2)),
     ]
     if reduce:
+        unit = rows_each // 2
         scratch += [
-            pltpu.VMEM((2 * seq, rows_each, half), BF16),
-            pltpu.VMEM((2 * seq, rows_each, half), BF16),
-            pltpu.VMEM((seq, rows_each, half), BF16),
-            pltpu.VMEM((seq, rows_each, half), BF16),
-            pltpu.VMEM((seq - 1, rows_each, half), BF16),
-            pltpu.VMEM((seq - 1, rows_each, half), BF16),
-            pltpu.VMEM((rows_each, half), F32),
+            pltpu.VMEM((16, unit, half), BF16),
+            pltpu.VMEM((16, unit, half), BF16),
+            pltpu.VMEM((8, unit, half), BF16),
+            pltpu.VMEM((8, unit, half), BF16),
+            pltpu.VMEM((6, unit, half), BF16),
+            pltpu.VMEM((6, unit, half), BF16),
+            pltpu.VMEM((2, unit, half), F32),
             pltpu.VMEM((4, rows_each, half), BF16),
-            dma((2 * seq,)),
-            dma((2 * seq,)),
-            dma((seq,)),
-            dma((seq,)),
-            dma((seq - 1,)),
-            dma((seq - 1,)),
-            dma((3,)),
-            dma((3,)),
+            dma((16,)),
+            dma((16,)),
+            dma((8,)),
+            dma((8,)),
+            dma((6,)),
+            dma((6,)),
+            dma((2, 3)),
+            dma((2, 3)),
             dma((4,)),
         ]
     grad, wgrad = pl.pallas_call(

time: 99 us -> 96.7 us (0.977)
  Pallas kernels: 98.1 us -> 95.8 us
    pallas_call x1, Pallas kernels: 95.4 us -> 93.1 us  [on_device(): pl.pallas_call(functools.partial(kernel, seq, spans, factor, early), out_...]
where the time goes in v4:
time: 96.7 us; the launch traced here: 96.5 us
  Pallas kernels  95.8 us (99%)
    pallas_call x1, Pallas kernels, on_device(): pl.pallas_call(functools.partial(kernel, seq, spans, factor, early), out_...  93.1 us
    pallas_call x1, Pallas kernels, on_device(): pl.pallas_call(finish, out_shape=shapes, in_specs=[anywhere, anywhere], o...  2.73 us

profile of v4, /device:TPU:1, one launch (start us, length us, event | category | flops | bytes accessed | tf_op | source)
XLA Modules:
  0.0 96.5 jit_solution(12506876395494692675)
XLA Ops:
  0.6 93.1 %shard_map.86 = (bf16[768,512]{1,0:T(8,128)(2,1)}, bf16[4,288,384]{2,1,0:T(8,128)(2,1)}) custom-call(bf16[192,2048]{1,0:T(8,128)(2,1)} %bitcast.4, bf16[768,512]{1,0:T(8,128)(2,1)} %bitcast.5, bf16[768,512]{1,0:T(8,128)(2,1)} %bitcast.6, bf16[3,768,768]{2,1,0:T(8,128)(2,1)} %w1_hbm.1, bf16[3,768,768]{2,1,0:T(8,128)(2,1)} %w2_hbm.1, f32[768]{0:T(1024)} %c1_ref.1, ...), custom_call_target="tpu_custom_call" | custom-call | flops 5435817984 | bytes 20000000 | tf_op jit(solution)/shard_map/pallas_call | solution.py:537
  93.7 2.7 %shard_map.87 = (bf16[768,512]{1,0:T(8,128)(2,1)}, f32[576,768]{1,0:T(8,128)}) custom-call(bf16[768,512]{1,0:T(8,128)(2,1)} %get-tuple-element.6.grad_hbm, bf16[4,288,384]{2,1,0:T(8,128)(2,1)} %get-tuple-element.7.parts_hbm), custom_call_target="tpu_custom_call" | custom-call | tf_op jit(solution)/shard_map/pallas_call | solution.py:559

commit v5 on v4

--- a/solution.py
+++ b/solution.py
@@ -223,21 +223,11 @@
     def border_terms(tap, side, has):
         @pl.when(has)
         def _():
-            for q in range(CHUNKS):
-                border_copy(q, side).wait_recv()
             tap_terms(tap, side)
 
         @pl.when(jnp.logical_not(has))
         def _():
             terms[pl.ds(tap * chan, chan), :] = jnp.zeros((chan, terms.shape[1]), F32)
-
-    tap_terms(1, 1)
-    if early is not None:
-        reduction = Reduction(z, x, core, sib, across, early, terms, more)
-        reduction.start_early()
-    border_terms(0, 2, sends_up)
-    border_terms(2, 0, sends_down)
-    load1.wait()
 
     def store_total(cols):
         def store(rows, value):
@@ -256,15 +246,23 @@
         )
         result_copy(q).start()
 
+    tap_terms(1, 1)
     if early is not None:
-        def first_layer_part(part):
-            for q in range(part * CHUNKS // 2, (part + 1) * CHUNKS // 2):
-                first_layer(q)
-
-        reduction.run(first_layer_part, wgrad_hbm)
+        reduction = Reduction(z, x, core, sib, across, early, terms, more)
+        reduction.start_early()
+    load1.wait()
+    for q in range(CHUNKS):
+        pl.when(sends_down)(border_copy(q, 0).wait_recv)
+        pl.when(sends_up)(border_copy(q, 2).wait_recv)
+        if q < CHUNKS - 1:
+            first_layer(q)
+    border_terms(0, 2, sends_up)
+    border_terms(2, 0, sends_down)
+
+    if early is not None:
+        reduction.run(functools.partial(first_layer, CHUNKS - 1), wgrad_hbm)
     else:
-        for q in range(CHUNKS):
-            first_layer(q)
+        first_layer(CHUNKS - 1)
         terms_out = pltpu.make_async_copy(terms, wgrad_hbm, w_sem.at[0])
         terms_out.start()
         terms_out.wait()
@@ -395,10 +393,9 @@
                     self.to_x(turn, k, self.block(k))
             for k in units:
                 self.to_core(turn, 4 + k, self.block(k), self.x)
-        meanwhile(0)
+        meanwhile()
         self.stage(0, 3)
         self.stage(0, 2)
-        meanwhile(1)
         self.stage(0, 1)
         self.stage(0, 0)
         self.stage(1, 3)

time: 96.7 us -> 96 us (level)
  no operation moved by 1% of the time
where the time goes in v5:
time: 96 us; the launch traced here: 95.8 us
  Pallas kernels  95.1 us (99%)
    pallas_call x1, Pallas kernels, on_device(): pl.pallas_call(functools.partial(kernel, seq, spans, factor, early), out_...  92.4 us
    pallas_call x1, Pallas kernels, on_device(): pl.pallas_call(finish, out_shape=shapes, in_specs=[anywhere, anywhere], o...  2.73 us

profile of v5, /device:TPU:1, one launch (start us, length us, event | category | flops | bytes accessed | tf_op | source)
XLA Modules:
  0.0 95.8 jit_solution(17437825087183186539)
XLA Ops:
  0.6 92.4 %shard_map.86 = (bf16[768,512]{1,0:T(8,128)(2,1)}, bf16[4,288,384]{2,1,0:T(8,128)(2,1)}) custom-call(bf16[192,2048]{1,0:T(8,128)(2,1)} %bitcast.4, bf16[768,512]{1,0:T(8,128)(2,1)} %bitcast.5, bf16[768,512]{1,0:T(8,128)(2,1)} %bitcast.6, bf16[3,768,768]{2,1,0:T(8,128)(2,1)} %w1_hbm.1, bf16[3,768,768]{2,1,0:T(8,128)(2,1)} %w2_hbm.1, f32[768]{0:T(1024)} %c1_ref.1, ...), custom_call_target="tpu_custom_call" | custom-call | flops 5435817984 | bytes 20000000 | tf_op jit(solution)/shard_map/pallas_call | solution.py:534
  93.0 2.7 %shard_map.87 = (bf16[768,512]{1,0:T(8,128)(2,1)}, f32[576,768]{1,0:T(8,128)}) custom-call(bf16[768,512]{1,0:T(8,128)(2,1)} %get-tuple-element.6.grad_hbm, bf16[4,288,384]{2,1,0:T(8,128)(2,1)} %get-tuple-element.7.parts_hbm), custom_call_target="tpu_custom_call" | custom-call | tf_op jit(solution)/shard_map/pallas_call | solution.py:556

commit v6 on v5

--- a/solution.py
+++ b/solution.py
@@ -210,24 +210,23 @@
         def _():
             border_copy(q, 2).start()
 
-    def tap_terms(tap, side):
-        @pl.loop(0, chan // BLOCK)
-        def _(step):
-            start = pl.multiple_of(step * BLOCK, BLOCK)
-            part = lax.dot_general(
-                gelu1[pl.ds(start, BLOCK), :], m[side],
-                (((1,), (1,)), ((), ())), preferred_element_type=F32,
-            )
-            terms[pl.ds(pl.multiple_of(tap * chan + start, BLOCK), BLOCK), :] = part * factor
-
-    def border_terms(tap, side, has):
+    def tap_terms(tap, side, cols, add):
+        part = lax.dot_general(
+            gelu1[:, cols], m[side, :, cols],
+            (((1,), (1,)), ((), ())), preferred_element_type=F32,
+        ) * factor
+        rows = pl.ds(tap * chan, chan)
+        terms[rows, :] = terms[rows, :] + part if add else part
+
+    def border_terms(tap, side, has, cols, add):
         @pl.when(has)
         def _():
-            tap_terms(tap, side)
-
-        @pl.when(jnp.logical_not(has))
-        def _():
-            terms[pl.ds(tap * chan, chan), :] = jnp.zeros((chan, terms.shape[1]), F32)
+            tap_terms(tap, side, cols, add)
+
+        if not add:
+            @pl.when(jnp.logical_not(has))
+            def _():
+                terms[pl.ds(tap * chan, chan), :] = jnp.zeros((chan, terms.shape[1]), F32)
 
     def store_total(cols):
         def store(rows, value):
@@ -246,7 +245,7 @@
         )
         result_copy(q).start()
 
-    tap_terms(1, 1)
+    tap_terms(1, 1, pl.ds(0, width), False)
     if early is not None:
         reduction = Reduction(z, x, core, sib, across, early, terms, more)
         reduction.start_early()
@@ -254,14 +253,18 @@
     for q in range(CHUNKS):
         pl.when(sends_down)(border_copy(q, 0).wait_recv)
         pl.when(sends_up)(border_copy(q, 2).wait_recv)
-        if q < CHUNKS - 1:
+        if q < CHUNKS - 2:
             first_layer(q)
-    border_terms(0, 2, sends_up)
-    border_terms(2, 0, sends_down)
+        else:
+            add = q == CHUNKS - 1
+            cols = pl.ds(q * piece, piece) if add else pl.ds(0, (CHUNKS - 1) * piece)
+            border_terms(0, 2, sends_up, cols, add)
+            border_terms(2, 0, sends_down, cols, add)
 
     if early is not None:
-        reduction.run(functools.partial(first_layer, CHUNKS - 1), wgrad_hbm)
+        reduction.run(first_layer, wgrad_hbm)
     else:
+        first_layer(CHUNKS - 2)
         first_layer(CHUNKS - 1)
         terms_out = pltpu.make_async_copy(terms, wgrad_hbm, w_sem.at[0])
         terms_out.start()
@@ -393,9 +396,10 @@
                     self.to_x(turn, k, self.block(k))
             for k in units:
                 self.to_core(turn, 4 + k, self.block(k), self.x)
-        meanwhile()
+        meanwhile(CHUNKS - 2)
         self.stage(0, 3)
         self.stage(0, 2)
+        meanwhile(CHUNKS - 1)
         self.stage(0, 1)
         self.stage(0, 0)
         self.stage(1, 3)

time: 96 us -> 95.6 us (level)
  no operation moved by 1% of the time
where the time goes in v6:
time: 95.6 us; the launch traced here: 95.4 us
  Pallas kernels  94.6 us (99%)
    pallas_call x1, Pallas kernels, on_device(): pl.pallas_call(functools.partial(kernel, seq, spans, factor, early), out_...  91.9 us
    pallas_call x1, Pallas kernels, on_device(): pl.pallas_call(finish, out_shape=shapes, in_specs=[anywhere, anywhere], o...  2.73 us

profile of v6, /device:TPU:1, one launch (start us, length us, event | category | flops | bytes accessed | tf_op | source)
XLA Modules:
  0.0 95.4 jit_solution(10808106741950025066)
XLA Ops:
  0.6 91.9 %shard_map.86 = (bf16[768,512]{1,0:T(8,128)(2,1)}, bf16[4,288,384]{2,1,0:T(8,128)(2,1)}) custom-call(bf16[192,2048]{1,0:T(8,128)(2,1)} %bitcast.4, bf16[768,512]{1,0:T(8,128)(2,1)} %bitcast.5, bf16[768,512]{1,0:T(8,128)(2,1)} %bitcast.6, bf16[3,768,768]{2,1,0:T(8,128)(2,1)} %w1_hbm.1, bf16[3,768,768]{2,1,0:T(8,128)(2,1)} %w2_hbm.1, f32[768]{0:T(1024)} %c1_ref.1, ...), custom_call_target="tpu_custom_call" | custom-call | flops 5435817984 | bytes 20000000 | tf_op jit(solution)/shard_map/pallas_call | solution.py:538
  92.5 2.7 %shard_map.87 = (bf16[768,512]{1,0:T(8,128)(2,1)}, f32[576,768]{1,0:T(8,128)}) custom-call(bf16[768,512]{1,0:T(8,128)(2,1)} %get-tuple-element.6.grad_hbm, bf16[4,288,384]{2,1,0:T(8,128)(2,1)} %get-tuple-element.7.parts_hbm), custom_call_target="tpu_custom_call" | custom-call | tf_op jit(solution)/shard_map/pallas_call | solution.py:560

commit v7 on v6

--- a/solution.py
+++ b/solution.py
@@ -19,6 +19,7 @@
 BF16 = jnp.bfloat16
 MESH = pl.DeviceIdType.MESH
 CHUNKS = 4
+AHEAD = 2
 STRIP = 64
 BLOCK = 768
 
@@ -144,7 +145,7 @@
                 else:
                     pl.when(valid(side, dest, span_second))(go)
 
-    for q in range(CHUNKS):
+    for q in range(AHEAD):
         each_share(q, lambda copy: copy.start(), False)
 
     own = pl.ds(pl.multiple_of(z * share, 16), share)
@@ -192,6 +193,8 @@
 
     for q in range(CHUNKS):
         each_share(q, lambda copy: copy.wait_recv(), True)
+        if q + AHEAD < CHUNKS:
+            each_share(q + AHEAD, lambda copy: copy.start(), False)
         cols = pl.ds(q * piece, piece)
 
         def store_middle(rows, value):

time: 95.6 us -> 95.8 us (level)
  no operation moved by 1% of the time
where the time goes in v7:
time: 95.8 us; the launch traced here: 95.6 us
  Pallas kernels  94.8 us (99%)
    pallas_call x1, Pallas kernels, on_device(): pl.pallas_call(functools.partial(kernel, seq, spans, factor, early), out_...  92.1 us
    pallas_call x1, Pallas kernels, on_device(): pl.pallas_call(finish, out_shape=shapes, in_specs=[anywhere, anywhere], o...  2.73 us

profile of v7, /device:TPU:1, one launch (start us, length us, event | category | flops | bytes accessed | tf_op | source)
XLA Modules:
  0.0 95.6 jit_solution(14058108834987275206)
XLA Ops:
  0.6 92.1 %shard_map.86 = (bf16[768,512]{1,0:T(8,128)(2,1)}, bf16[4,288,384]{2,1,0:T(8,128)(2,1)}) custom-call(bf16[192,2048]{1,0:T(8,128)(2,1)} %bitcast.4, bf16[768,512]{1,0:T(8,128)(2,1)} %bitcast.5, bf16[768,512]{1,0:T(8,128)(2,1)} %bitcast.6, bf16[3,768,768]{2,1,0:T(8,128)(2,1)} %w1_hbm.1, bf16[3,768,768]{2,1,0:T(8,128)(2,1)} %w2_hbm.1, f32[768]{0:T(1024)} %c1_ref.1, ...), custom_call_target="tpu_custom_call" | custom-call | flops 5435817984 | bytes 20000000 | tf_op jit(solution)/shard_map/pallas_call | solution.py:541
  92.7 2.7 %shard_map.87 = (bf16[768,512]{1,0:T(8,128)(2,1)}, f32[576,768]{1,0:T(8,128)}) custom-call(bf16[768,512]{1,0:T(8,128)(2,1)} %get-tuple-element.6.grad_hbm, bf16[4,288,384]{2,1,0:T(8,128)(2,1)} %get-tuple-element.7.parts_hbm), custom_call_target="tpu_custom_call" | custom-call | tf_op jit(solution)/shard_map/pallas_call | solution.py:563
